TPU v7x, 32 devices: a whole 2x2x4 slice. The times are simulated.
32 devices in a mesh: dp: 8 (over z, y), ctx: 4 (over x, core).
Axes of the slice: x: 2, y: 2, z: 4, core: 2. Of those that a mesh axis runs over, the one named last changes fastest.
Arguments:
- queries: bfloat16 [8, 512, 4096], P('dp', 'ctx'), may hold values from -160 to 160
- keys: bfloat16 [8, 512, 512], P('dp', 'ctx'), may hold values from -6 to 6
- values: bfloat16 [8, 512, 512], P('dp', 'ctx'), may hold values from -6 to 6
- doc_start: int32 [8, 512], P('dp', 'ctx'), may hold values from -256 to 511, as said below
Outputs:
- attended: bfloat16 [8, 512, 4096], P('dp', 'ctx')
Inputs may be any that keep to these rules, and one draw needn't show every extreme that they name: A document that begins before its slab does so in the slab before, at place -256 or later; in slab 0 every document begins at 0 or later. doc_start never decreases along sequence places, and each token's document begins at or before the token.
All inputs are finite; a program needn't handle non-finite values.
Results may differ from a plain program's by a relative error of at most 0.0035.
Values may be sent and summed in bfloat16 or wider, within the bound.
A program may use at most 64 MiB of HBM per device.

v0:
```python
import math

import jax
import jax.numpy as jnp
from jax import lax
from jax.sharding import PartitionSpec as P

H = 32
KVH = 4
HD = 128


ROPE_BASE = 500000.0
NEG_FILL = -1e30


def from_behind(block, axis, distance):
    devices = range(lax.axis_size(axis))
    route = [(i - distance, i) for i in devices if i - distance in devices]
    return lax.ppermute(block, axis, route)


def rotate(field, rel_pos, head_count, head_width):
    half_width = head_width // 2
    inv_freq = ROPE_BASE ** (-2.0 * jnp.arange(half_width, dtype=jnp.float32) / head_width)
    angles = rel_pos.astype(jnp.float32)[:, None] * inv_freq[None, :]
    cosine = jnp.cos(angles)[:, None, :]
    sine = jnp.sin(angles)[:, None, :]
    shaped = field.astype(jnp.float32).reshape(field.shape[0], head_count, head_width)
    first_half = shaped[..., :half_width]
    second_half = shaped[..., half_width:]
    result = jnp.concatenate(
        [first_half * cosine - second_half * sine, second_half * cosine + first_half * sine],
        axis=-1,
    )
    return result.reshape(field.shape[0], head_count * head_width).astype(jnp.bfloat16)


def key_positions(key_index, key_width, offset, tok_rows, ctx_count, slab_span):
    half_rows = tok_rows // 2
    owner = key_index // key_width
    row_in = key_index % key_width + offset
    base_pos = (
        jnp.where(row_in < half_rows, owner, 2 * ctx_count - 1 - owner) * half_rows
        + row_in % half_rows
    )
    return base_pos - jnp.where(row_in >= tok_rows, slab_span, 0)


def attend(softmax_state, piece, key_pos, q_split, q_pos, q_start, score_scale):
    piece_rows = piece.shape[0]
    block_rows = math.gcd(piece_rows, 512)
    block_count = piece_rows // block_rows
    head_feats = KVH * HD

    def one_block(block_id, current):
        kv_block = lax.dynamic_slice_in_dim(piece, block_id * block_rows, block_rows, 0)
        pos_block = lax.dynamic_slice_in_dim(key_pos, block_id * block_rows, block_rows, 0)
        k_block = kv_block[:, :head_feats].reshape(block_rows, KVH, HD)
        v_block = kv_block[:, head_feats:].reshape(block_rows, KVH, HD).astype(jnp.float32)
        maxima, totals, accums = ([], [], [])
        for which_half in range(2):
            allowed = (pos_block[None, :] <= q_pos[which_half][:, None]) & (
                pos_block[None, :] >= q_start[which_half][:, None]
            )
            queries_half = q_split[which_half]

            def update(operands):
                run_max, run_sum, run_acc = operands
                scores = (
                    jnp.einsum(
                        "qkgd,nkd->kgqn", queries_half, k_block, preferred_element_type=jnp.float32
                    )
                    * score_scale
                )
                scores = jnp.where(allowed[None, None], scores, NEG_FILL)
                new_max = jnp.maximum(run_max, jnp.max(scores, axis=-1))
                weights = jnp.where(allowed[None, None], jnp.exp(scores - new_max[..., None]), 0.0)
                rescale = jnp.exp(run_max - new_max)
                new_sum = run_sum * rescale + jnp.sum(weights, axis=-1)
                new_acc = run_acc * rescale[..., None] + jnp.einsum(
                    "kgqn,nkd->kgqd", weights, v_block, precision=lax.Precision.HIGHEST
                )
                return (new_max, new_sum, new_acc)

            updated = lax.cond(
                jnp.any(allowed),
                update,
                lambda operands: operands,
                (current[0][which_half], current[1][which_half], current[2][which_half]),
            )
            maxima.append(updated[0])
            totals.append(updated[1])
            accums.append(updated[2])
        return (jnp.stack(maxima), jnp.stack(totals), jnp.stack(accums))

    return lax.fori_loop(0, block_count, one_block, softmax_state)


def per_device(queries, keys, values, doc_start):
    ctx_count = lax.axis_size("ctx")
    device = lax.axis_index("ctx")
    tok_rows = queries.shape[1]
    half_rows = tok_rows // 2
    slab_span = tok_rows * ctx_count
    groups = H // KVH
    score_scale = HD ** (-0.5)
    row_index = jnp.arange(tok_rows, dtype=jnp.int32)
    stretch_index = jnp.where(row_index < half_rows, device, 2 * ctx_count - 1 - device)
    positions = stretch_index * half_rows + row_index % half_rows
    starts = doc_start[0]
    rel_pos = positions - starts
    q_rot = rotate(queries[0], rel_pos, H, HD)
    k_rot = rotate(keys[0], rel_pos, KVH, HD)
    kv_own = jnp.concatenate([k_rot, values[0]], axis=1)
    carried = from_behind(kv_own[half_rows:], "dp", 1)
    q_split = q_rot.reshape(2, half_rows, KVH, groups, HD)
    q_pos = positions.reshape(2, half_rows)
    q_start = starts.reshape(2, half_rows)
    softmax_state = (
        jnp.full((2, KVH, groups, half_rows), NEG_FILL, jnp.float32),
        jnp.zeros((2, KVH, groups, half_rows), jnp.float32),
        jnp.zeros((2, KVH, groups, half_rows, HD), jnp.float32),
    )

    def folder(key_width, offset, current, piece):
        key_index = jnp.arange(piece.shape[0], dtype=jnp.int32)
        key_pos = key_positions(key_index, key_width, offset, tok_rows, ctx_count, slab_span)
        return attend(current, piece, key_pos, q_split, q_pos, q_start, score_scale)

    softmax_state = folder(
        tok_rows, 0, softmax_state, lax.all_gather(kv_own, "ctx", axis=0, tiled=True)
    )
    softmax_state = folder(
        half_rows, tok_rows, softmax_state, lax.all_gather(carried, "ctx", axis=0, tiled=True)
    )
    mixed = softmax_state[2] / softmax_state[1][..., None]
    mixed = mixed.transpose(0, 3, 1, 2, 4).reshape(tok_rows, H * HD)
    return mixed.astype(jnp.bfloat16)[None]


def solution(mesh):
    return jax.shard_map(
        per_device,
        mesh=mesh,
        in_specs=(P("dp", "ctx", None), P("dp", "ctx", None), P("dp", "ctx", None), P("dp", "ctx")),
        out_specs=P("dp", "ctx", None),
        check_vma=False,
    )
```

profile of v0, /device:TPU:12, one launch (start us, length us, event | category | flops | bytes accessed | tf_op | source)
XLA Modules:
  0.0 81.1 jit_solution(14805423044910837168)
XLA Ops:
  6.6 1.1 %copy.26 = bf16[1,128,512]{1,2,0:T(8,128)(2,1)S(1)} copy(bf16[1,128,512]{2,1,0:T(8,128)(2,1)} %param.14) | data formatting | bytes 262144 | tf_op args[2]
  7.7 1.0 %copy.67 = f32[1,128,512]{1,2,0:T(8,128)S(1)} copy(bf16[1,128,512]{2,1,0:T(8,128)(2,1)} %param.13) | data formatting | bytes 393216 | tf_op jit(solution)/shard_map/convert_element_type | solution.py:29
  11.2 3.4 %collective-permute-start = (bf16[64,1024]{0,1:T(8,128)(2,1)}, bf16[64,1024]{0,1:T(8,128)(2,1)}, u32[]{:S(2)}, u32[]{:S(2)}) collective-permute-start(bf16[64,1024]{0,1:T(8,128)(2,1)} %fusion.65), channel_id=1, source_target_pairs={{0,4},{4,8},{8,12},{12,16},{16,20},{20,24},{24,28},{1,5},{5,9},{9,... | collective-permute-start | bytes 393224 | tf_op jit(solution)/shard_map/ppermute | solution.py:20
  20.9 2.4 %subtract_convert_fusion = (bf16[128,32,64]{2,0,1:T(8,128)(2,1)S(1)}, bf16[128,32,64]{2,0,1:T(8,128)(2,1)S(1)}) fusion(f32[128,32,64]{2,1,0:T(8,128)S(1)} %get-tuple-element.336, f32[128,32,64]{2,1,0:T(8,128)S(1)} %get-tuple-element.335, f32[128,64]{1,0:T(8,128)S(1)} %copy.30, f32[128,64]{1,0:T(8,128)S(1)} %copy.28), kind=kLoop, calls=%fused_computation.82 | loop fusion | flops 2097152 | bytes 3211264 | tf_op jit(solution)/shard_map/convert.4
  23.3 1.6 %fusion.64 = (bf16[64,32,128]{2,0,1:T(8,128)(2,1)}, bf16[64,32,128]{2,0,1:T(8,128)(2,1)}) fusion(bf16[128,32,64]{2,0,1:T(8,128)(2,1)S(1)} %get-tuple-element.331, bf16[128,32,64]{2,0,1:T(8,128)(2,1)S(1)} %get-tuple-element.332), kind=kLoop, calls=%fused_computation.86 | loop fusion | flops 2097152 | bytes 2097152 | tf_op jit(solution)/shard_map/concatenate | solution.py:32
  25.0 1.1 %copy.33 = bf16[64,1024]{1,0:T(8,128)(2,1)S(1)} copy(bf16[64,1024]{0,1:T(8,128)(2,1)} %collective-permute-done) | data formatting | bytes 262144 | tf_op jit(solution)/shard_map/ppermute | solution.py:20
  26.1 7.2 %all_gather.7 = bf16[256,1024]{1,0:T(8,128)(2,1)S(1)} all-gather(bf16[64,1024]{1,0:T(8,128)(2,1)S(1)} %copy.33), channel_id=1, replica_groups=mesh['dp'=8,'ctx'=4] {'ctx'}, dimensions={0}, use_global_device_ids=true | all-gather | bytes 655360 | tf_op jit(solution)/shard_map/all_gather | solution.py:135
  33.6 1.3 %fusion.93 = (bf16[512,512]{0,1:T(8,128)(2,1)S(1)}, bf16[512,512]{0,1:T(8,128)(2,1)S(1)}) fusion(bf16[512,1024]{0,1:T(8,128)(2,1)} %all-gather.2.cloned.1.call-done), kind=kLoop, calls=%fused_computation.152 | loop fusion | bytes 2097152 | tf_op jit(solution)/shard_map/while/body/eval_jaxpr/slice | solution.py:60
  34.9 1.1 %convert.20 = f32[512,4,128]{0,2,1:T(8,128)} convert(bf16[512,4,128]{0,2,1:T(8,128)(2,1)S(1)} %bitcast.150) | non-fusion elementwise | flops 262144 | bytes 1572864 | tf_op jit(solution)/shard_map/while/body/eval_jaxpr/convert_element_type | solution.py:60
  36.0 11.4 %conditional.6 = (f32[4,8,64]{2,1,0:T(8,128)}, f32[4,8,64]{2,1,0:T(8,128)S(1)}, f32[4,8,64,128]{3,2,1,0:T(8,128)S(1)}) conditional(s32[]{:T(128)} %convert_element_type.87, (f32[4,8,64]{2,1,0:T(8,128)S(1)}, f32[4,8,64]{2,1,0:T(8,128)S(1)}, f32[4,8,64,128]{3,2,1,0:T(8,128)S(1)}) %tuple.75, (pred[64,512]{1,0:T(8,128)(4,1)S(1)}, ...), branch_computations={%region_12.13_spmd, %region_13.16_spmd} | conditional | flops 1892159488 | bytes 16990232 | solution.py:86
  36.0 1.8 %fusion.31 = (f32[4,8,64]{2,1,0:T(8,128)S(1)}, f32[4,512,64,8]{1,2,3,0:T(8,128)S(1)}) fusion(pred[64,512]{1,0:T(8,128)(4,1)S(1)} %get-tuple-element.212, bf16[64,4,8,128]{3,0,2,1:T(8,128)(2,1)} %get-tuple-element.214, bf16[512,4,128]{0,2,1:T(8,128)(2,1)S(1)} %get-tuple-element.296), kind=kOutput, calls=%fused_computation.41 | convolution fusion | flops 271579136 | bytes 5283840 | tf_op jit(solution)/shard_map/while/body/eval_jaxpr/cond/branch_1_fun/qkgd,nkd->kgqn/dot_general | solution.py:71
  38.5 2.0 %fusion.33 = f32[4,8,64]{2,1,0:T(8,128)S(1)} fusion(f32[4,512,64,8]{1,2,3,0:T(8,128)S(1)} %get-tuple-element.328, f32[4,8,64]{2,1,0:T(8,128)} %max.12, pred[64,512]{1,0:T(8,128)(4,1)S(1)} %get-tuple-element.212), kind=kLoop, calls=%fused_computation.43 | loop fusion | flops 5240832 | bytes 4243456 | tf_op jit(solution)/shard_map/while/body/eval_jaxpr/cond/branch_1_fun/reduce_sum | solution.py:80
  41.2 6.2 %fusion.39 = f32[4,8,64,128]{3,2,1,0:T(8,128)S(1)} fusion(f32[4,512,64,8]{1,2,3,0:T(8,128)S(1)} %get-tuple-element.328, f32[4,8,64]{2,1,0:T(8,128)} %max.12, pred[64,512]{1,0:T(8,128)(4,1)S(1)} %get-tuple-element.212, f32[512,4,128]{0,2,1:T(8,128)} %get-tuple-element.301, f32[4,8,64,128]{3,2,1,0:T(8,128)S(1)} %get-tuple-element.216, ...), kind=kOutput, calls=%fused_computation.49 | convolution fusion | flops 1615331328 | bytes 7389184 | tf_op jit(solution)/shard_map/while/body/eval_jaxpr/cond/branch_1_fun/kgqn,nkd->kgqd/dot_general | solution.py:81
  47.4 11.6 %conditional.4 = (f32[4,8,64]{2,1,0:T(8,128)}, f32[4,8,64]{2,1,0:T(8,128)S(1)}, f32[4,8,64,128]{3,2,1,0:T(8,128)S(1)}) conditional(s32[]{:T(128)} %convert_element_type.75, (f32[4,8,64]{2,1,0:T(8,128)S(1)}, f32[4,8,64]{2,1,0:T(8,128)S(1)}, f32[4,8,64,128]{3,2,1,0:T(8,128)S(1)}) %tuple.75, (pred[64,512]{1,0:T(8,128)(4,1)S(1)}, ...), branch_computations={%region_2.3_spmd, %region_3.6_spmd} | conditional | flops 1892159488 | bytes 16990232 | solution.py:86
  47.6 1.8 %fusion = (f32[4,8,64]{2,1,0:T(8,128)S(1)}, f32[4,512,64,8]{1,2,3,0:T(8,128)S(1)}) fusion(pred[64,512]{1,0:T(8,128)(4,1)S(1)} %get-tuple-element.198, bf16[64,4,8,128]{3,0,2,1:T(8,128)(2,1)} %get-tuple-element.200, bf16[512,4,128]{0,2,1:T(8,128)(2,1)S(1)} %get-tuple-element.282), kind=kOutput, calls=%fused_computation.2 | convolution fusion | flops 271579136 | bytes 5283840 | tf_op jit(solution)/shard_map/while/body/eval_jaxpr/cond/branch_1_fun/qkgd,nkd->kgqn/dot_general | solution.py:71
  50.1 2.0 %fusion.2 = f32[4,8,64]{2,1,0:T(8,128)S(1)} fusion(f32[4,512,64,8]{1,2,3,0:T(8,128)S(1)} %get-tuple-element.324, f32[4,8,64]{2,1,0:T(8,128)} %max.10, pred[64,512]{1,0:T(8,128)(4,1)S(1)} %get-tuple-element.198), kind=kLoop, calls=%fused_computation.4 | loop fusion | flops 5240832 | bytes 4243456 | tf_op jit(solution)/shard_map/while/body/eval_jaxpr/cond/branch_1_fun/reduce_sum | solution.py:80
  52.9 6.2 %fusion.8 = f32[4,8,64,128]{3,2,1,0:T(8,128)S(1)} fusion(f32[4,512,64,8]{1,2,3,0:T(8,128)S(1)} %get-tuple-element.324, f32[4,8,64]{2,1,0:T(8,128)} %max.10, pred[64,512]{1,0:T(8,128)(4,1)S(1)} %get-tuple-element.198, f32[512,4,128]{0,2,1:T(8,128)} %get-tuple-element.287, f32[4,8,64,128]{3,2,1,0:T(8,128)S(1)} %get-tuple-element.202, ...), kind=kOutput, calls=%fused_computation.10 | convolution fusion | flops 1615331328 | bytes 7389184 | tf_op jit(solution)/shard_map/while/body/eval_jaxpr/cond/branch_1_fun/kgqn,nkd->kgqd/dot_general | solution.py:81
  59.0 6.7 %conditional.7 = (f32[1,4,8,64,128]{4,3,2,1,0:T(8,128)S(1)}, f32[1,4,8,64]{3,2,1,0:T(8,128)S(1)}) conditional(s32[]{:T(128)} %convert_element_type.86, (f32[4,8,64]{2,1,0:T(8,128)S(1)}, f32[4,8,64,128]{3,2,1,0:T(8,128)S(1)}) %tuple.132, (pred[64,256]{1,0:T(8,128)(4,1)S(1)}, bf16[256,4,128]{0,2,1:T(8,128)(2,1)S(1)}, ...), branch_computations={%region_16.17_spmd, %region_17.20_spmd} | conditional | flops 946343936 | bytes 9863184 | solution.py:86
  59.1 1.6 %fusion.46 = (f32[4,8,64]{2,1,0:T(8,128)S(1)}, f32[4,256,64,8]{1,2,3,0:T(8,128)S(1)}) fusion(pred[64,256]{1,0:T(8,128)(4,1)S(1)} %get-tuple-element.220, bf16[64,4,8,128]{3,0,2,1:T(8,128)(2,1)} %get-tuple-element.222, bf16[256,4,128]{0,2,1:T(8,128)(2,1)S(1)} %get-tuple-element.303), kind=kOutput, calls=%fused_computation.60 | convolution fusion | flops 135788544 | bytes 2908160 | tf_op jit(solution)/shard_map/while/body/eval_jaxpr/cond/branch_1_fun/qkgd,nkd->kgqn/dot_general | solution.py:71
  61.4 0.9 %fusion.48 = f32[4,8,64]{2,1,0:T(8,128)S(1)} fusion(f32[4,256,64,8]{1,2,3,0:T(8,128)S(1)} %get-tuple-element.330, f32[4,8,64]{2,1,0:T(8,128)S(1)} %max.13, pred[64,256]{1,0:T(8,128)(4,1)S(1)} %get-tuple-element.220), kind=kLoop, calls=%fused_computation.62 | loop fusion | flops 2619392 | bytes 2129920 | tf_op jit(solution)/shard_map/while/body/eval_jaxpr/cond/branch_1_fun/reduce_sum | solution.py:80
  63.1 2.6 %fusion.50 = f32[1,4,8,64,128]{4,3,2,1,0:T(8,128)S(1)} fusion(f32[4,256,64,8]{1,2,3,0:T(8,128)S(1)} %get-tuple-element.330, f32[4,8,64,128]{3,2,1,0:T(8,128)S(1)} %get-tuple-element.223, f32[4,8,64]{2,1,0:T(8,128)S(1)} %max.13, pred[64,256]{1,0:T(8,128)(4,1)S(1)} %get-tuple-element.220, f32[256,4,128]{0,2,1:T(8,128)S(1)} %get-tuple-element.308, ...), kind=kOutput, calls=%fused_computation.64 | convolution fusion | flops 807927808 | bytes 4751360 | tf_op jit(solution)/shard_map/while/body/eval_jaxpr/cond/branch_1_fun/kgqn,nkd->kgqd/dot_general | solution.py:81
  65.7 5.8 %conditional.5 = (f32[1,4,8,64,128]{4,3,2,1,0:T(8,128)S(1)}, f32[1,4,8,64]{3,2,1,0:T(8,128)S(1)}) conditional(s32[]{:T(128)} %convert_element_type.74, (f32[4,8,64]{2,1,0:T(8,128)S(1)}, f32[4,8,64,128]{3,2,1,0:T(8,128)S(1)}) %tuple.130, (pred[64,256]{1,0:T(8,128)(4,1)S(1)}, bf16[256,4,128]{0,2,1:T(8,128)(2,1)S(1)}, ...), branch_computations={%region_6.7_spmd, %region_7.10_spmd} | conditional | flops 946343936 | bytes 9863184 | solution.py:86
  68.9 2.6 %fusion.19 = f32[1,4,8,64,128]{4,3,2,1,0:T(8,128)S(1)} fusion(f32[4,256,64,8]{1,2,3,0:T(8,128)S(1)} %get-tuple-element.326, f32[4,8,64,128]{3,2,1,0:T(8,128)S(1)} %get-tuple-element.209, f32[4,8,64]{2,1,0:T(8,128)S(1)} %max.11, pred[64,256]{1,0:T(8,128)(4,1)S(1)} %get-tuple-element.206, f32[256,4,128]{0,2,1:T(8,128)S(1)} %get-tuple-element.294, ...), kind=kOutput, calls=%fused_computation.25 | convolution fusion | flops 807927808 | bytes 4751360 | tf_op jit(solution)/shard_map/while/body/eval_jaxpr/cond/branch_1_fun/kgqn,nkd->kgqd/dot_general | solution.py:81
  73.0 1.3 %convert_element_type.90 = bf16[1,128,4096]{2,1,0:T(8,128)(2,1)} reshape(bf16[2,64,4,8,128]{4,3,2,1,0:T(8,128)(2,1)S(1)} %copy.42) | data formatting | bytes 2097152 | tf_op jit(solution)/shard_map/convert_element_type | solution.py:139
  (48 shorter events, 14.8 us)
Async XLA Ops:
  6.5 8.1 %copy-start.2 = (s32[1,128]{1,0:T(1,128)S(1)}, s32[1,128]{1,0:T(1,128)}, u32[]{:S(2)}) copy-start(s32[1,128]{1,0:T(1,128)} %param.15) | copy-start | bytes 1540
  6.5 11.6 %copy-start.1 = (bf16[1,128,4096]{2,1,0:T(8,128)(2,1)S(1)}, bf16[1,128,4096]{2,1,0:T(8,128)(2,1)}, u32[]{:S(2)}) copy-start(bf16[1,128,4096]{2,1,0:T(8,128)(2,1)} %param.12) | copy-start | bytes 3145732
  6.5 27.1 %all-gather.2.cloned.1.call-start = ((), (), s32[]{:S(2)}) async-start(), calls=%async_computation | async-start | bytes 1310720 | tf_op jit(solution)/shard_map/all_gather | solution.py:132
  11.2 13.8 %collective-permute-start = (bf16[64,1024]{0,1:T(8,128)(2,1)}, bf16[64,1024]{0,1:T(8,128)(2,1)}, u32[]{:S(2)}, u32[]{:S(2)}) collective-permute-start(bf16[64,1024]{0,1:T(8,128)(2,1)} %fusion.65), channel_id=1, source_target_pairs={{0,4},{4,8},{8,12},{12,16},{16,20},{20,24},{24,28},{1,5},{5,9},{9,... | collective-permute-start | bytes 393224 | tf_op jit(solution)/shard_map/ppermute | solution.py:20
  59.0 6.7 %copy-start = (bf16[64,32,128]{2,0,1:T(8,128)(2,1)S(1)}, bf16[64,32,128]{2,0,1:T(8,128)(2,1)}, u32[]{:S(2)}) copy-start(bf16[64,32,128]{2,0,1:T(8,128)(2,1)} %get-tuple-element.333) | copy-start | bytes 1572868
Sparse Core Ops, SparseCore 0:
  10.5 17.9 all-gather.1
where the time goes:
time: 82.7 us; the launch traced here: 81.1 us
  matrix products  23.4 us (28%)
  other arithmetic  21.9 us (26%)
  between operations  16.3 us (20%)
  local copies, waits for them, and re-layouts  8.27 us (10%)
  blocking collectives  7.17 us (9%)
  starting transfers between devices  3.42 us (4%)
    dot_general x4, matrix products, update(): jnp.einsum('kgqn,nkd->kgqd', weights, v_block, precision=lax.Precision.HI...  17.6 us
    all_gather x1, blocking collectives, per_device(): lax.all_gather(carried, 'ctx', axis=0, tiled=True)  7.17 us
    reduce_sum x4, other arithmetic, update(): new_sum = run_sum * rescale + jnp.sum(weights, axis=-1)  5.92 us
    dot_general x4, matrix products, update(): jnp.einsum('qkgd,nkd->kgqn', queries_half, k_block, preferred_element_typ...  5.83 us
    ppermute x1, starting transfers between devices, from_behind(): return lax.ppermute(block, axis, route)  3.42 us
    max x4, other arithmetic, update(): new_max = jnp.maximum(run_max, jnp.max(scores, axis=-1))  2.67 us
    another operation x2, other arithmetic  2.49 us
    convert_element_type x2, local copies, waits for them, and re-layouts, per_device(): return mixed.astype(jnp.bfloat16)[None]  1.95 us
  transfers between devices with their start and end apart: 2, of which 0 were waited for; matrix products, arithmetic and copies ran while one was open for 12% of the time, Pallas kernels for 0%

commit v1 on v0

v1 whole, which is shorter than its diff:
```python
import functools
import math

import jax
import jax.numpy as jnp
import numpy as np
from jax import lax
from jax.experimental import pallas as pl
from jax.experimental.pallas import tpu as pltpu
from jax.sharding import PartitionSpec as P

H = 32
KVH = 4
HD = 128
ROPE_BASE = 500000.0
FILL = -1e30
MESH = pl.DeviceIdType.MESH
C2 = HD ** (-0.5) * math.log2(math.e)


def cos_sin(angles, want_cos):
    n = jnp.floor(angles * (2.0 / math.pi) + 0.5)
    r = ((angles - n * 1.5703125) - n * 4.837512969970703125e-4) - n * 7.54978995489188216e-8
    z = r * r
    s = ((-1.9515295891e-4 * z + 8.3321608736e-3) * z - 1.6666654611e-1) * z * r + r
    c = ((2.443315711809948e-5 * z - 1.388731625493765e-3) * z + 4.166664568298827e-2) * z * z - 0.5 * z + 1.0
    quadrant = n.astype(jnp.int32) + jnp.where(want_cos, 1, 0)
    v = jnp.where((quadrant & 1) == 1, c, s)
    return jnp.where((quadrant & 2) == 2, -v, v)


def kernel(n_ctx, n_dp, q_hbm, k_hbm, v_hbm, ds_hbm, freq_hbm, o_hbm,
           q_in, k_in, ds_in, freq_in, kv, q_rot, bias, m_st, acc, o_buf,
           in_sem, out_sem, recv_sem, fwd_sem, lo_sem, hi_sem, ca_sem, dp_sem):
    N = n_ctx
    d = lax.axis_index("dp")
    c = lax.axis_index("ctx")
    sib = c + 1 - 2 * (c % 2)
    half = q_in.shape[0] // 2
    feats = KVH * HD
    groups = H // KVH
    peers = [lax.rem(c + 2 * t, N) for t in range(1, N // 2)]
    slot_lo = N + c
    slot_hi = 3 * N - 1 - c
    slot_ca = N - 1 - c

    cp_ds = pltpu.make_async_copy(ds_hbm, ds_in, in_sem.at[0])
    cp_fr = pltpu.make_async_copy(freq_hbm, freq_in, in_sem.at[1])
    cp_k = pltpu.make_async_copy(k_hbm.at[0], k_in, in_sem.at[2])
    cp_v0 = pltpu.make_async_copy(v_hbm.at[0, pl.ds(0, half)], kv.at[slot_lo, :, pl.ds(feats, feats)], in_sem.at[3])
    cp_v1 = pltpu.make_async_copy(v_hbm.at[0, pl.ds(half, half)], kv.at[slot_hi, :, pl.ds(feats, feats)], in_sem.at[4])
    cp_q = pltpu.make_async_copy(q_hbm.at[0], q_in, in_sem.at[5])
    for cp in (cp_ds, cp_fr, cp_k, cp_v0, cp_v1, cp_q):
        cp.start()

    barrier = pltpu.get_barrier_semaphore()
    pl.semaphore_signal(barrier, inc=1, device_id=(d, sib), device_id_type=MESH)
    for p in peers:
        pl.semaphore_signal(barrier, inc=1, device_id=(d, p), device_id_type=MESH)

    @pl.when(d > 0)
    def _():
        pl.semaphore_signal(barrier, inc=1, device_id=(d - 1, c), device_id_type=MESH)

    cp_ds.wait()
    cp_fr.wait()
    tok = 2 * half
    starts = jnp.transpose(jnp.broadcast_to(ds_in[...].astype(jnp.float32), (HD, tok)))
    row = lax.broadcasted_iota(jnp.int32, (tok, HD), 0)
    lane = lax.broadcasted_iota(jnp.int32, (tok, HD), 1)
    pos = jnp.where(row < half, c * half + row, (2 * N - 2 - c) * half + row)
    posf = pos.astype(jnp.float32)
    low_lane = lane < HD // 2
    trig = cos_sin((posf - starts) * freq_in[...], low_lane)
    trig_r = pltpu.roll(trig, HD // 2, 1)
    cosine = jnp.where(low_lane, trig, trig_r)
    sine = jnp.where(low_lane, -trig_r, trig)

    cp_k.wait()
    for h in range(KVH):
        x = k_in[:, h * HD:(h + 1) * HD].astype(jnp.float32)
        y = (x * cosine + pltpu.roll(x, HD // 2, 1) * sine).astype(jnp.bfloat16)
        kv[slot_lo, :, h * HD:(h + 1) * HD] = y[:half]
        kv[slot_hi, :, h * HD:(h + 1) * HD] = y[half:]
    cp_v0.wait()
    cp_v1.wait()

    has_next = jnp.where(d < n_dp - 1, 1, 0)
    pl.semaphore_wait(barrier, N // 2 + has_next)

    def push(src_slot, dst_slot, send, dev):
        return pltpu.make_async_remote_copy(
            src_ref=kv.at[src_slot], dst_ref=kv.at[dst_slot], send_sem=send,
            recv_sem=recv_sem.at[dst_slot], device_id=dev, device_id_type=MESH)

    def got(slot):
        push(slot, slot, fwd_sem.at[slot], (d, sib)).wait_recv()

    def forward(slot):
        push(slot, slot, fwd_sem.at[slot], (d, sib)).start()

    to_dp = push(slot_hi, slot_ca, dp_sem.at[0], (d + 1, c))

    @pl.when(d < n_dp - 1)
    def _():
        to_dp.start()

    for t, p in enumerate(peers):
        push(slot_lo, slot_lo, lo_sem.at[t], (d, p)).start()

        @pl.when(p < c)
        def _():
            push(slot_hi, slot_hi, hi_sem.at[t], (d, p)).start()

    forward(slot_lo)

    @pl.when(sib < c)
    def _():
        forward(slot_hi)

    def clear(slot):
        kv[slot] = jnp.zeros(kv.shape[1:], kv.dtype)

    for s in range(2 * N, 3 * N):
        @pl.when(s > slot_hi)
        def _():
            clear(s)

    @pl.when(d == 0)
    def _():
        for s in range(N):
            clear(s)

    for s in range(0, 3 * N * half, 128):
        key = (lane + (s - N * half)).astype(jnp.float32)
        bias[:, s:s + 128] = jnp.where((key <= posf) & (key >= starts), 0.0, FILL)

    cp_q.wait()
    for h in range(H):
        x = q_in[:, h * HD:(h + 1) * HD].astype(jnp.float32)
        y = (x * cosine + pltpu.roll(x, HD // 2, 1) * sine).astype(jnp.bfloat16)
        g = h % groups
        q_rot[h // groups, g * half:(g + 1) * half] = y[:half]
        q_rot[h // groups, (groups + g) * half:(groups + g + 1) * half] = y[half:]

    for p in peers:
        got(N + p)
        forward(N + p)

        @pl.when(p > c)
        def _():
            got(3 * N - 1 - p)
            forward(3 * N - 1 - p)

    @pl.when(d > 0)
    def _():
        got(slot_ca)
        for t, p in enumerate(peers):
            push(slot_ca, slot_ca, ca_sem.at[t], (d, p)).start()
        forward(slot_ca)

    got(N + sib)

    @pl.when(sib > c)
    def _():
        got(3 * N - 1 - sib)
    for p in peers:
        ps = p + 1 - 2 * (p % 2)
        got(N + ps)

        @pl.when(p > c)
        def _():
            got(3 * N - 1 - ps)

    rows = groups * half
    ones = jnp.ones((N * half, HD), jnp.bfloat16)

    def piece(kvh, which, base, first):
        col = pl.multiple_of(kvh * HD, HD)
        vcol = pl.multiple_of(feats + kvh * HD, HD)
        k = kv[base:base + N, :, pl.ds(col, HD)].reshape(N * half, HD)
        v = kv[base:base + N, :, pl.ds(vcol, HD)].reshape(N * half, HD)
        va = jnp.concatenate([v, ones], axis=1)
        for w in which:
            r0 = w * rows
            q = q_rot[kvh, r0:r0 + rows]
            s = lax.dot_general(q, k, (((1,), (1,)), ((), ())), preferred_element_type=jnp.float32)
            b = bias[w * half:(w + 1) * half, base * half:(base + N) * half]
            s = s.reshape(groups, half, N * half) * C2 + b[None]
            top = jnp.max(s, axis=-1, keepdims=True).reshape(rows, 1)
            if not first:
                old = m_st[kvh, r0:r0 + rows]
                new = jnp.maximum(old, top)
                scale = jnp.exp2(old - new)
                top = new[:, :1]
            else:
                new = jnp.broadcast_to(top, (rows, HD))
            m_st[kvh, r0:r0 + rows] = new
            wide = jnp.concatenate([new] * (N * half // HD), axis=1)
            w_bf = jnp.exp2(s.reshape(rows, N * half) - wide).astype(jnp.bfloat16)
            pv = jnp.dot(w_bf, va, preferred_element_type=jnp.float32)
            if not first:
                pv = pv + acc[kvh, r0:r0 + rows] * jnp.concatenate([scale, scale], axis=1)
            acc[kvh, r0:r0 + rows] = pv

    def low_high(kvh, _):
        piece(kvh, (0, 1), N, True)
        piece(kvh, (1,), 2 * N, False)
        return _

    lax.fori_loop(0, KVH, low_high, 0)

    @pl.when(d > 0)
    def _():
        for p in peers:
            got(N - 1 - p)
            forward(N - 1 - p)
        got(N - 1 - sib)
        for p in peers:
            ps = p + 1 - 2 * (p % 2)
            got(N - 1 - ps)

    def carried(kvh, _):
        piece(kvh, (0, 1), 0, False)
        for w in range(2):
            for g in range(groups):
                r0 = w * rows + g * half
                a = acc[kvh, r0:r0 + half]
                o = (a[:, :HD] / a[:, HD:]).astype(jnp.bfloat16)
                o_buf[kvh, w * half:(w + 1) * half, g * HD:(g + 1) * HD] = o
        pltpu.make_async_copy(o_buf.at[kvh], o_hbm.at[0, :, pl.ds(pl.multiple_of(kvh * groups * HD, HD), groups * HD)], out_sem.at[kvh]).start()
        return _

    lax.fori_loop(0, KVH, carried, 0)

    for kvh in range(KVH):
        pltpu.make_async_copy(o_buf.at[kvh], o_hbm.at[0, :, pl.ds(kvh * groups * HD, groups * HD)], out_sem.at[kvh]).wait()

    def sent(slot, sem):
        push(slot, slot, sem, (d, sib)).wait_send()

    for t, p in enumerate(peers):
        sent(slot_lo, lo_sem.at[t])
        sent(N + p, fwd_sem.at[N + p])

        @pl.when(p < c)
        def _():
            sent(slot_hi, hi_sem.at[t])

        @pl.when(p > c)
        def _():
            sent(3 * N - 1 - p, fwd_sem.at[3 * N - 1 - p])

        @pl.when(d > 0)
        def _():
            sent(slot_ca, ca_sem.at[t])
            sent(N - 1 - p, fwd_sem.at[N - 1 - p])
    sent(slot_lo, fwd_sem.at[slot_lo])

    @pl.when(sib < c)
    def _():
        sent(slot_hi, fwd_sem.at[slot_hi])

    @pl.when(d > 0)
    def _():
        sent(slot_ca, fwd_sem.at[slot_ca])

    @pl.when(d < n_dp - 1)
    def _():
        sent(slot_hi, dp_sem.at[0])


def solution(mesh):
    n_ctx = mesh.shape["ctx"]
    n_dp = mesh.shape["dp"]
    freq = ROPE_BASE ** (-2.0 * np.arange(HD // 2, dtype=np.float64) / HD)
    freq = np.concatenate([freq, freq]).astype(np.float32)[None]

    def per_device(queries, keys, values, doc_start):
        tok = queries.shape[1]
        half = tok // 2
        groups = H // KVH
        np_half = max(n_ctx // 2 - 1, 1)
        hbm = pl.BlockSpec(memory_space=pl.ANY)
        return pl.pallas_call(
            functools.partial(kernel, n_ctx, n_dp),
            out_shape=jax.ShapeDtypeStruct(queries.shape, jnp.bfloat16),
            in_specs=[hbm] * 5,
            out_specs=hbm,
            scratch_shapes=[
                pltpu.VMEM((tok, H * HD), jnp.bfloat16),
                pltpu.VMEM((tok, KVH * HD), jnp.bfloat16),
                pltpu.VMEM((1, tok), jnp.int32),
                pltpu.VMEM((1, HD), jnp.float32),
                pltpu.VMEM((3 * n_ctx, half, 2 * KVH * HD), jnp.bfloat16),
                pltpu.VMEM((KVH, groups * tok, HD), jnp.bfloat16),
                pltpu.VMEM((tok, 3 * n_ctx * half), jnp.float32),
                pltpu.VMEM((KVH, groups * tok, HD), jnp.float32),
                pltpu.VMEM((KVH, groups * tok, 2 * HD), jnp.float32),
                pltpu.VMEM((KVH, tok, groups * HD), jnp.bfloat16),
                pltpu.SemaphoreType.DMA((6,)),
                pltpu.SemaphoreType.DMA((KVH,)),
                pltpu.SemaphoreType.DMA((3 * n_ctx,)),
                pltpu.SemaphoreType.DMA((3 * n_ctx,)),
                pltpu.SemaphoreType.DMA((np_half,)),
                pltpu.SemaphoreType.DMA((np_half,)),
                pltpu.SemaphoreType.DMA((np_half,)),
                pltpu.SemaphoreType.DMA((1,)),
            ],
            compiler_params=pltpu.CompilerParams(
                collective_id=0, has_side_effects=True, vmem_limit_bytes=48 * 1024 * 1024
            ),
        )(queries, keys, values, doc_start, jnp.asarray(freq))

    return jax.shard_map(
        per_device,
        mesh=mesh,
        in_specs=(P("dp", "ctx", None), P("dp", "ctx", None), P("dp", "ctx", None), P("dp", "ctx")),
        out_specs=P("dp", "ctx", None),
        check_vma=False,
    )
```

time: 82.7 us -> 24.3 us (0.29)
  the two profiles are of different devices: /device:TPU:12 before, /device:TPU:8 now
where the time goes in v1:
time: 24.3 us; the launch traced here: 24.1 us
  Pallas kernels  18.8 us (77%)
  local copies, waits for them, and re-layouts  5.31 us (22%)
    pallas_call x1, Pallas kernels, per_device(): pl.pallas_call(functools.partial(kernel, n_ctx, n_dp), out_shape=jax.Shap...  18.8 us
    unnamed x11, local copies, waits for them, and re-layouts  5.31 us

profile of v1, /device:TPU:8, one launch (start us, length us, event | category | flops | bytes accessed | tf_op | source)
XLA Modules:
  0.0 24.1 jit_solution(9324415013911198366)
XLA Ops:
  0.0 0.0 copy-start
  0.0 1.2 %copy-done = bf16[1,128,4096]{2,1,0:T(8,128)(2,1)S(1)} copy-done((bf16[1,128,4096]{2,1,0:T(8,128)(2,1)S(1)}, bf16[1,128,4096]{2,1,0:T(8,128)(2,1)}, u32[]{:S(2)}) %copy-start) | copy-done | bytes 1048600
  1.2 0.0 copy-start.1
  1.2 0.9 %copy-done.1 = bf16[1,128,512]{2,1,0:T(8,128)(2,1)S(1)} copy-done((bf16[1,128,512]{2,1,0:T(8,128)(2,1)S(1)}, bf16[1,128,512]{2,1,0:T(8,128)(2,1)}, u32[]{:S(2)}) %copy-start.1) | copy-done | bytes 131096
  2.1 0.0 copy-start.2
  2.1 0.9 %copy-done.2 = bf16[1,128,512]{2,1,0:T(8,128)(2,1)S(1)} copy-done((bf16[1,128,512]{2,1,0:T(8,128)(2,1)S(1)}, bf16[1,128,512]{2,1,0:T(8,128)(2,1)}, u32[]{:S(2)}) %copy-start.2) | copy-done | bytes 131096
  3.0 0.0 copy-start.3
  3.0 0.7 %copy-done.3 = s32[1,128]{1,0:T(1,128)S(1)} copy-done((s32[1,128]{1,0:T(1,128)S(1)}, s32[1,128]{1,0:T(1,128)}, u32[]{:S(2)}) %copy-start.3) | copy-done | bytes 536
  3.7 0.0 copy-start.4
  3.7 0.7 %copy-done.4 = f32[1,128]{1,0:T(1,128)S(1)} copy-done((f32[1,128]{1,0:T(1,128)S(1)}, f32[1,128]{1,0:T(1,128)}, u32[]{:S(2)}) %copy-start.4) | copy-done | bytes 536
  4.3 18.8 %shard_map.55 = bf16[1,128,4096]{2,1,0:T(8,128)(2,1)S(1)} custom-call(bf16[1,128,4096]{2,1,0:T(8,128)(2,1)S(1)} %copy-done, bf16[1,128,512]{2,1,0:T(8,128)(2,1)S(1)} %copy-done.1, bf16[1,128,512]{2,1,0:T(8,128)(2,1)S(1)} %copy-done.2, s32[1,128]{1,0:T(1,128)S(1)} %copy-done.3, f32[1,128]{1,0:T(1,128)S(1)} %copy-done.4), custom_call_target="tpu_custom_call" | custom-call | tf_op jit(solution)/shard_map/pallas_call | solution.py:285
  23.1 1.0 %copy.7 = bf16[1,128,4096]{2,1,0:T(8,128)(2,1)} copy(bf16[1,128,4096]{2,1,0:T(8,128)(2,1)S(1)} %shard_map.55) | data formatting | bytes 2097152
Async XLA Ops:
  0.0 1.2 %copy-start = (bf16[1,128,4096]{2,1,0:T(8,128)(2,1)S(1)}, bf16[1,128,4096]{2,1,0:T(8,128)(2,1)}, u32[]{:S(2)}) copy-start(bf16[1,128,4096]{2,1,0:T(8,128)(2,1)} %q_hbm.1) | copy-start | bytes 3145732
  1.2 0.9 %copy-start.1 = (bf16[1,128,512]{2,1,0:T(8,128)(2,1)S(1)}, bf16[1,128,512]{2,1,0:T(8,128)(2,1)}, u32[]{:S(2)}) copy-start(bf16[1,128,512]{2,1,0:T(8,128)(2,1)} %k_hbm.1) | copy-start | bytes 393220
  2.1 0.9 %copy-start.2 = (bf16[1,128,512]{2,1,0:T(8,128)(2,1)S(1)}, bf16[1,128,512]{2,1,0:T(8,128)(2,1)}, u32[]{:S(2)}) copy-start(bf16[1,128,512]{2,1,0:T(8,128)(2,1)} %v_hbm.1) | copy-start | bytes 393220
  3.0 0.7 %copy-start.3 = (s32[1,128]{1,0:T(1,128)S(1)}, s32[1,128]{1,0:T(1,128)}, u32[]{:S(2)}) copy-start(s32[1,128]{1,0:T(1,128)} %ds_hbm.1) | copy-start | bytes 1540
  3.7 0.7 %copy-start.4 = (f32[1,128]{1,0:T(1,128)S(1)}, f32[1,128]{1,0:T(1,128)}, u32[]{:S(2)}) copy-start(f32[1,128]{1,0:T(1,128)} %constant.2.clone.freq_hbm) | copy-start | bytes 1540

commit v2 on v1

--- a/solution.py
+++ b/solution.py
@@ -106,11 +106,12 @@
         to_dp.start()
 
     for t, p in enumerate(peers):
+        @pl.when(p < c)
+        def _():
+            push(slot_hi, slot_hi, hi_sem.at[t], (d, p)).start()
+
+    for t, p in enumerate(peers):
         push(slot_lo, slot_lo, lo_sem.at[t], (d, p)).start()
-
-        @pl.when(p < c)
-        def _():
-            push(slot_hi, slot_hi, hi_sem.at[t], (d, p)).start()
 
     forward(slot_lo)
 
@@ -143,34 +144,31 @@
         q_rot[h // groups, g * half:(g + 1) * half] = y[:half]
         q_rot[h // groups, (groups + g) * half:(groups + g + 1) * half] = y[half:]
 
+    for t, p in enumerate(peers):
+        @pl.when(p > c)
+        def _():
+            got(3 * N - 1 - p)
+            forward(3 * N - 1 - p)
+
+            @pl.when(d < n_dp - 1)
+            def _():
+                push(3 * N - 1 - p, N - 1 - p, dp_sem.at[1 + t], (d + 1, c)).start()
+
+    @pl.when(d > 0)
+    def _():
+        got(slot_ca)
+        for t, p in enumerate(peers):
+            @pl.when(p > c)
+            def _():
+                push(slot_ca, slot_ca, ca_sem.at[t], (d, p)).start()
+        forward(slot_ca)
+
     for p in peers:
         got(N + p)
         forward(N + p)
-
-        @pl.when(p > c)
-        def _():
-            got(3 * N - 1 - p)
-            forward(3 * N - 1 - p)
-
-    @pl.when(d > 0)
-    def _():
-        got(slot_ca)
-        for t, p in enumerate(peers):
-            push(slot_ca, slot_ca, ca_sem.at[t], (d, p)).start()
-        forward(slot_ca)
-
     got(N + sib)
-
-    @pl.when(sib > c)
-    def _():
-        got(3 * N - 1 - sib)
     for p in peers:
-        ps = p + 1 - 2 * (p % 2)
-        got(N + ps)
-
-        @pl.when(p > c)
-        def _():
-            got(3 * N - 1 - ps)
+        got(N + p + 1 - 2 * (p % 2))
 
     rows = groups * half
     ones = jnp.ones((N * half, HD), jnp.bfloat16)
@@ -203,22 +201,37 @@
                 pv = pv + acc[kvh, r0:r0 + rows] * jnp.concatenate([scale, scale], axis=1)
             acc[kvh, r0:r0 + rows] = pv
 
-    def low_high(kvh, _):
+    def low(kvh, _):
         piece(kvh, (0, 1), N, True)
+        return _
+
+    def high(kvh, _):
         piece(kvh, (1,), 2 * N, False)
         return _
 
-    lax.fori_loop(0, KVH, low_high, 0)
+    lax.fori_loop(0, KVH, low, 0)
 
     @pl.when(d > 0)
     def _():
         for p in peers:
             got(N - 1 - p)
             forward(N - 1 - p)
+
+    @pl.when(sib > c)
+    def _():
+        got(3 * N - 1 - sib)
+    for p in peers:
+        @pl.when(p > c)
+        def _():
+            got(3 * N - 1 - (p + 1 - 2 * (p % 2)))
+
+    lax.fori_loop(0, KVH, high, 0)
+
+    @pl.when(d > 0)
+    def _():
         got(N - 1 - sib)
         for p in peers:
-            ps = p + 1 - 2 * (p % 2)
-            got(N - 1 - ps)
+            got(N - 1 - (p + 1 - 2 * (p % 2)))
 
     def carried(kvh, _):
         piece(kvh, (0, 1), 0, False)
@@ -251,9 +264,16 @@
         def _():
             sent(3 * N - 1 - p, fwd_sem.at[3 * N - 1 - p])
 
+            @pl.when(d < n_dp - 1)
+            def _():
+                sent(3 * N - 1 - p, dp_sem.at[1 + t])
+
+            @pl.when(d > 0)
+            def _():
+                sent(slot_ca, ca_sem.at[t])
+
         @pl.when(d > 0)
         def _():
-            sent(slot_ca, ca_sem.at[t])
             sent(N - 1 - p, fwd_sem.at[N - 1 - p])
     sent(slot_lo, fwd_sem.at[slot_lo])
 
@@ -286,7 +306,7 @@
             functools.partial(kernel, n_ctx, n_dp),
             out_shape=jax.ShapeDtypeStruct(queries.shape, jnp.bfloat16),
             in_specs=[hbm] * 5,
-            out_specs=hbm,
+            out_specs=pl.BlockSpec(memory_space=pl.ANY),
             scratch_shapes=[
                 pltpu.VMEM((tok, H * HD), jnp.bfloat16),
                 pltpu.VMEM((tok, KVH * HD), jnp.bfloat16),
@@ -305,10 +325,10 @@
                 pltpu.SemaphoreType.DMA((np_half,)),
                 pltpu.SemaphoreType.DMA((np_half,)),
                 pltpu.SemaphoreType.DMA((np_half,)),
-                pltpu.SemaphoreType.DMA((1,)),
+                pltpu.SemaphoreType.DMA((1 + np_half,)),
             ],
             compiler_params=pltpu.CompilerParams(
-                collective_id=0, has_side_effects=True, vmem_limit_bytes=48 * 1024 * 1024
+                collective_id=0, has_side_effects=True, vmem_limit_bytes=63 * 1024 * 1024
             ),
         )(queries, keys, values, doc_start, jnp.asarray(freq))
 

time: 24.3 us -> 22 us (0.905)
  the two profiles are of different devices: /device:TPU:8 before, /device:TPU:1 now
where the time goes in v2:
time: 22 us; the launch traced here: 21.9 us
  Pallas kernels  19.6 us (89%)
  local copies, waits for them, and re-layouts  2.29 us (10%)
    pallas_call x1, Pallas kernels, per_device(): pl.pallas_call(functools.partial(kernel, n_ctx, n_dp), out_shape=jax.Shap...  19.6 us
    unnamed x1, local copies, waits for them, and re-layouts  2.29 us

profile of v2, /device:TPU:1, one launch (start us, length us, event | category | flops | bytes accessed | tf_op | source)
XLA Modules:
  0.0 21.9 jit_solution(17167212007844376145)
XLA Ops:
  0.0 19.6 %shard_map.55 = bf16[1,128,4096]{2,1,0:T(8,128)(2,1)} custom-call(bf16[1,128,4096]{2,1,0:T(8,128)(2,1)} %q_hbm.1, bf16[1,128,512]{2,1,0:T(8,128)(2,1)} %k_hbm.1, bf16[1,128,512]{2,1,0:T(8,128)(2,1)} %v_hbm.1, s32[1,128]{1,0:T(1,128)} %ds_hbm.1, f32[1,128]{1,0:T(1,128)} %constant.2.clone.freq_hbm), custom_call_target="tpu_custom_call" | custom-call | tf_op jit(solution)/shard_map/pallas_call | solution.py:305
  19.6 2.3 %copy.7 = bf16[1,128,4096]{2,1,0:T(8,128)(2,1)} copy(bf16[1,128,4096]{2,1,0:T(8,128)(2,1)} %shard_map.55) | data formatting | bytes 2097152

commit v3 on v2

--- a/solution.py
+++ b/solution.py
@@ -209,7 +209,7 @@
         piece(kvh, (1,), 2 * N, False)
         return _
 
-    lax.fori_loop(0, KVH, low, 0)
+    lax.fori_loop(0, KVH, low, 0, unroll=True)
 
     @pl.when(d > 0)
     def _():
@@ -225,7 +225,7 @@
         def _():
             got(3 * N - 1 - (p + 1 - 2 * (p % 2)))
 
-    lax.fori_loop(0, KVH, high, 0)
+    lax.fori_loop(0, KVH, high, 0, unroll=True)
 
     @pl.when(d > 0)
     def _():
@@ -244,7 +244,7 @@
         pltpu.make_async_copy(o_buf.at[kvh], o_hbm.at[0, :, pl.ds(pl.multiple_of(kvh * groups * HD, HD), groups * HD)], out_sem.at[kvh]).start()
         return _
 
-    lax.fori_loop(0, KVH, carried, 0)
+    lax.fori_loop(0, KVH, carried, 0, unroll=True)
 
     for kvh in range(KVH):
         pltpu.make_async_copy(o_buf.at[kvh], o_hbm.at[0, :, pl.ds(kvh * groups * HD, groups * HD)], out_sem.at[kvh]).wait()
@@ -328,9 +328,9 @@
                 pltpu.SemaphoreType.DMA((1 + np_half,)),
             ],
             compiler_params=pltpu.CompilerParams(
-                collective_id=0, has_side_effects=True, vmem_limit_bytes=63 * 1024 * 1024
+                collective_id=0, has_side_effects=True, vmem_limit_bytes=48 * 1024 * 1024
             ),
-        )(queries, keys, values, doc_start, jnp.asarray(freq))
+        )(*[pltpu.with_memory_space_constraint(x, pltpu.HBM) for x in (queries, keys, values, doc_start, jnp.asarray(freq))])
 
     return jax.shard_map(
         per_device,

time: 22 us -> 18 us (0.82)
  Pallas kernels: 19.6 us -> 16.8 us
  local copies, waits for them, and re-layouts: 2.29 us -> 0.97 us
    pallas_call x1, Pallas kernels: 19.6 us -> 16.8 us  [per_device(): pl.pallas_call(functools.partial(kernel, n_ctx, n_dp), out_shape=jax.Shap...]
    unnamed x1, local copies, waits for them, and re-layouts: 2.29 us -> 0.97 us
where the time goes in v3:
time: 18 us; the launch traced here: 17.8 us
  Pallas kernels  16.8 us (93%)
  local copies, waits for them, and re-layouts  0.97 us (5%)
    pallas_call x1, Pallas kernels, per_device(): pl.pallas_call(functools.partial(kernel, n_ctx, n_dp), out_shape=jax.Shap...  16.8 us
    unnamed x1, local copies, waits for them, and re-layouts  0.97 us

profile of v3, /device:TPU:1, one launch (start us, length us, event | category | flops | bytes accessed | tf_op | source)
XLA Modules:
  0.0 17.8 jit_solution(9174076128891523329)
XLA Ops:
  0.0 16.8 %shard_map.55 = bf16[1,128,4096]{2,1,0:T(8,128)(2,1)S(1)} custom-call(bf16[1,128,4096]{2,1,0:T(8,128)(2,1)} %q_hbm.1, bf16[1,128,512]{2,1,0:T(8,128)(2,1)} %k_hbm.1, bf16[1,128,512]{2,1,0:T(8,128)(2,1)} %v_hbm.1, s32[1,128]{1,0:T(1,128)} %ds_hbm.1, f32[1,128]{1,0:T(1,128)} %constant.2.clone.freq_hbm), custom_call_target="tpu_custom_call" | custom-call | tf_op jit(solution)/shard_map/pallas_call | solution.py:305
  16.8 1.0 %copy.7 = bf16[1,128,4096]{2,1,0:T(8,128)(2,1)} copy(bf16[1,128,4096]{2,1,0:T(8,128)(2,1)S(1)} %shard_map.55) | data formatting | bytes 2097152

commit v4 on v3

--- a/solution.py
+++ b/solution.py
@@ -14,6 +14,23 @@
 HD = 128
 ROPE_BASE = 500000.0
 FILL = -1e30
+class Parts:
+    def __init__(self, copies):
+        self.copies = copies
+
+    def start(self):
+        for copy in self.copies:
+            copy.start()
+
+    def wait_recv(self):
+        for copy in self.copies:
+            copy.wait_recv()
+
+    def wait_send(self):
+        for copy in self.copies:
+            copy.wait_send()
+
+
 MESH = pl.DeviceIdType.MESH
 C2 = HD ** (-0.5) * math.log2(math.e)
 
@@ -88,16 +105,19 @@
     has_next = jnp.where(d < n_dp - 1, 1, 0)
     pl.semaphore_wait(barrier, N // 2 + has_next)
 
-    def push(src_slot, dst_slot, send, dev):
-        return pltpu.make_async_remote_copy(
-            src_ref=kv.at[src_slot], dst_ref=kv.at[dst_slot], send_sem=send,
-            recv_sem=recv_sem.at[dst_slot], device_id=dev, device_id_type=MESH)
-
-    def got(slot):
-        push(slot, slot, fwd_sem.at[slot], (d, sib)).wait_recv()
-
-    def forward(slot):
-        push(slot, slot, fwd_sem.at[slot], (d, sib)).start()
+    part = half // 2
+
+    def push(src_slot, dst_slot, send, dev, parts=(0, 1)):
+        return Parts([pltpu.make_async_remote_copy(
+            src_ref=kv.at[src_slot, pl.ds(i * part, part)], dst_ref=kv.at[dst_slot, pl.ds(i * part, part)],
+            send_sem=send.at[i], recv_sem=recv_sem.at[dst_slot, i], device_id=dev, device_id_type=MESH)
+            for i in parts])
+
+    def got(slot, parts=(0, 1)):
+        push(slot, slot, fwd_sem.at[slot], (d, sib), parts).wait_recv()
+
+    def forward(slot, parts=(0, 1)):
+        push(slot, slot, fwd_sem.at[slot], (d, sib), parts).start()
 
     to_dp = push(slot_hi, slot_ca, dp_sem.at[0], (d + 1, c))
 
@@ -144,24 +164,26 @@
         q_rot[h // groups, g * half:(g + 1) * half] = y[:half]
         q_rot[h // groups, (groups + g) * half:(groups + g + 1) * half] = y[half:]
 
-    for t, p in enumerate(peers):
-        @pl.when(p > c)
-        def _():
-            got(3 * N - 1 - p)
-            forward(3 * N - 1 - p)
-
-            @pl.when(d < n_dp - 1)
-            def _():
-                push(3 * N - 1 - p, N - 1 - p, dp_sem.at[1 + t], (d + 1, c)).start()
-
-    @pl.when(d > 0)
-    def _():
-        got(slot_ca)
+    for i in range(2):
+        @pl.when(d > 0)
+        def _():
+            got(slot_ca, (i,))
+            for t, p in enumerate(peers):
+                @pl.when(p > c)
+                def _():
+                    push(slot_ca, slot_ca, ca_sem.at[t], (d, p), (i,)).start()
+            forward(slot_ca, (i,))
+
         for t, p in enumerate(peers):
             @pl.when(p > c)
             def _():
-                push(slot_ca, slot_ca, ca_sem.at[t], (d, p)).start()
-        forward(slot_ca)
+                got(3 * N - 1 - p, (i,))
+
+                @pl.when(d < n_dp - 1)
+                def _():
+                    push(3 * N - 1 - p, N - 1 - p, dp_sem.at[1 + t], (d + 1, c), (i,)).start()
+
+                forward(3 * N - 1 - p, (i,))
 
     for p in peers:
         got(N + p)
@@ -320,12 +342,12 @@
                 pltpu.VMEM((KVH, tok, groups * HD), jnp.bfloat16),
                 pltpu.SemaphoreType.DMA((6,)),
                 pltpu.SemaphoreType.DMA((KVH,)),
-                pltpu.SemaphoreType.DMA((3 * n_ctx,)),
-                pltpu.SemaphoreType.DMA((3 * n_ctx,)),
-                pltpu.SemaphoreType.DMA((np_half,)),
-                pltpu.SemaphoreType.DMA((np_half,)),
-                pltpu.SemaphoreType.DMA((np_half,)),
-                pltpu.SemaphoreType.DMA((1 + np_half,)),
+                pltpu.SemaphoreType.DMA((3 * n_ctx, 2)),
+                pltpu.SemaphoreType.DMA((3 * n_ctx, 2)),
+                pltpu.SemaphoreType.DMA((np_half, 2)),
+                pltpu.SemaphoreType.DMA((np_half, 2)),
+                pltpu.SemaphoreType.DMA((np_half, 2)),
+                pltpu.SemaphoreType.DMA((1 + np_half, 2)),
             ],
             compiler_params=pltpu.CompilerParams(
                 collective_id=0, has_side_effects=True, vmem_limit_bytes=48 * 1024 * 1024

time: 18 us -> 18.2 us (1.011)
  Pallas kernels: 16.8 us -> 17.1 us
    pallas_call x1, Pallas kernels: 16.8 us -> 17.1 us  [per_device(): pl.pallas_call(functools.partial(kernel, n_ctx, n_dp), out_shape=jax.Shap...]
where the time goes in v4:
time: 18.2 us; the launch traced here: 18.1 us
  Pallas kernels  17.1 us (94%)
  local copies, waits for them, and re-layouts  0.97 us (5%)
    pallas_call x1, Pallas kernels, per_device(): pl.pallas_call(functools.partial(kernel, n_ctx, n_dp), out_shape=jax.Shap...  17.1 us
    unnamed x1, local copies, waits for them, and re-layouts  0.97 us

profile of v4, /device:TPU:1, one launch (start us, length us, event | category | flops | bytes accessed | tf_op | source)
XLA Modules:
  0.0 18.1 jit_solution(1627514638735528864)
XLA Ops:
  0.0 17.1 %shard_map.55 = bf16[1,128,4096]{2,1,0:T(8,128)(2,1)S(1)} custom-call(bf16[1,128,4096]{2,1,0:T(8,128)(2,1)} %q_hbm.1, bf16[1,128,512]{2,1,0:T(8,128)(2,1)} %k_hbm.1, bf16[1,128,512]{2,1,0:T(8,128)(2,1)} %v_hbm.1, s32[1,128]{1,0:T(1,128)} %ds_hbm.1, f32[1,128]{1,0:T(1,128)} %constant.2.clone.freq_hbm), custom_call_target="tpu_custom_call" | custom-call | tf_op jit(solution)/shard_map/pallas_call | solution.py:327
  17.1 1.0 %copy.7 = bf16[1,128,4096]{2,1,0:T(8,128)(2,1)} copy(bf16[1,128,4096]{2,1,0:T(8,128)(2,1)S(1)} %shard_map.55) | data formatting | bytes 2097152

commit v5 on v3

--- a/solution.py
+++ b/solution.py
@@ -144,16 +144,6 @@
         q_rot[h // groups, g * half:(g + 1) * half] = y[:half]
         q_rot[h // groups, (groups + g) * half:(groups + g + 1) * half] = y[half:]
 
-    for t, p in enumerate(peers):
-        @pl.when(p > c)
-        def _():
-            got(3 * N - 1 - p)
-            forward(3 * N - 1 - p)
-
-            @pl.when(d < n_dp - 1)
-            def _():
-                push(3 * N - 1 - p, N - 1 - p, dp_sem.at[1 + t], (d + 1, c)).start()
-
     @pl.when(d > 0)
     def _():
         got(slot_ca)
@@ -162,6 +152,16 @@
             def _():
                 push(slot_ca, slot_ca, ca_sem.at[t], (d, p)).start()
         forward(slot_ca)
+
+    for t, p in enumerate(peers):
+        @pl.when(p > c)
+        def _():
+            got(3 * N - 1 - p)
+            forward(3 * N - 1 - p)
+
+            @pl.when(d < n_dp - 1)
+            def _():
+                push(3 * N - 1 - p, N - 1 - p, dp_sem.at[1 + t], (d + 1, c)).start()
 
     for p in peers:
         got(N + p)

time: 18 us -> 18 us (level)
  no operation moved by 1% of the time
where the time goes in v5:
time: 18 us; the launch traced here: 17.8 us
  Pallas kernels  16.8 us (93%)
  local copies, waits for them, and re-layouts  0.97 us (5%)
    pallas_call x1, Pallas kernels, per_device(): pl.pallas_call(functools.partial(kernel, n_ctx, n_dp), out_shape=jax.Shap...  16.8 us
    unnamed x1, local copies, waits for them, and re-layouts  0.97 us

profile of v5, /device:TPU:1, one launch (start us, length us, event | category | flops | bytes accessed | tf_op | source)
XLA Modules:
  0.0 17.8 jit_solution(11990167098820632000)
XLA Ops:
  0.0 16.8 %shard_map.55 = bf16[1,128,4096]{2,1,0:T(8,128)(2,1)S(1)} custom-call(bf16[1,128,4096]{2,1,0:T(8,128)(2,1)} %q_hbm.1, bf16[1,128,512]{2,1,0:T(8,128)(2,1)} %k_hbm.1, bf16[1,128,512]{2,1,0:T(8,128)(2,1)} %v_hbm.1, s32[1,128]{1,0:T(1,128)} %ds_hbm.1, f32[1,128]{1,0:T(1,128)} %constant.2.clone.freq_hbm), custom_call_target="tpu_custom_call" | custom-call | tf_op jit(solution)/shard_map/pallas_call | solution.py:305
  16.8 1.0 %copy.7 = bf16[1,128,4096]{2,1,0:T(8,128)(2,1)} copy(bf16[1,128,4096]{2,1,0:T(8,128)(2,1)S(1)} %shard_map.55) | data formatting | bytes 2097152
